TPU v7x, 256 devices: a whole 4x4x8 slice. The times are simulated.
256 devices in a mesh: row: 8 (over y, x_hi), col: 32 (over z, x_lo, core).
Axes of the slice: x: 4 (x_hi: 2, x_lo: 2; x = x_hi * 2 + x_lo), y: 4, z: 8, core: 2. Of those that a mesh axis runs over, the one named last changes fastest.
Arguments:
- vectors: bfloat16 [8, 131072], P(None, ('col', 'row')), may hold values from -6 to 6
- energies: float32 [131072], P(('col', 'row')), may hold values from 0.5 to 3
- tiles: bfloat16 [8, 32, 256, 128, 128], P('row', 'col'), may hold values from -0.09375 to 0.09375
- tile_rows: int32 [8, 32, 256], P('row', 'col'), may hold values from 0 to 127, as said below
- tile_cols: int32 [8, 32, 256], P('row', 'col'), may hold values from 0 to 31
- counts: int32 [8, 32], P('row', 'col'), may hold values from 1 to 256, as said below
Outputs:
- product: bfloat16 [8, 131072], P(None, ('col', 'row'))
Inputs may be any that keep to these rules, and one draw needn't show every extreme that they name: `tile_rows`: a // 4 <= c on device (r, c), and I <= J for every slot: only the upper block triangle is stored. `counts`: slots at or past a device's count are ignored; some device has all 256 slots live.
All inputs are finite; a program needn't handle non-finite values.
Results may differ from a plain program's by a relative error of at most 0.0013.
Values may be sent and summed in bfloat16 or wider, within the bound.
A program may use at most 64 MiB of HBM per device.

v0:
```python
import jax
import jax.numpy as jnp
from jax import lax
from jax.sharding import PartitionSpec as P


def as_blocks(flat, width):
    return flat.reshape(flat.shape[0], -1, width).transpose(1, 0, 2)


def as_flat(blocks):
    return blocks.transpose(1, 0, 2).reshape(blocks.shape[1], -1)


def tile_pass(tiles, gather_index, target_index, source, nseg, live_count, transposed):

    def apply(block_tiles, picked):
        if transposed:
            return jnp.einsum(
                "tij,tvi->tvj", block_tiles, picked, preferred_element_type=jnp.float32
            )
        return jnp.einsum("tij,tvj->tvi", block_tiles, picked, preferred_element_type=jnp.float32)

    slots = tiles.shape[0]
    terms = apply(tiles, source[gather_index])
    live = (jnp.arange(slots) < live_count)[:, None, None]
    terms = jnp.where(live, terms, jnp.float32(0.0))
    return jax.ops.segment_sum(terms, target_index, nseg)


def reduce_slab(row_part):
    flat_part = as_flat(row_part)
    return lax.psum_scatter(flat_part, "col", scatter_dimension=1, tiled=True)


def reduce_segment(col_part):
    return lax.psum_scatter(as_flat(col_part), "row", scatter_dimension=1, tiled=True)


def fetch_slab(vectors):
    return lax.all_gather(vectors, "col", axis=1, tiled=True)


def body(vectors, energies, tiles, tile_rows, tile_cols, counts):
    width = tiles.shape[-1]
    slots = tiles.shape[2]
    local_tiles = tiles.reshape(slots, width, width)
    local_rows = tile_rows.reshape(slots)
    local_cols = tile_cols.reshape(slots)
    live_count = counts.reshape(())
    own_width = vectors.shape[1]
    segment = as_blocks(lax.all_gather(vectors, "row", axis=1, tiled=True), width)
    slab_blocks = lax.axis_size("col") * own_width // width
    segment_blocks = segment.shape[0]
    slab = as_blocks(fetch_slab(vectors), width)
    row_part = tile_pass(
        local_tiles, local_cols, local_rows, segment, slab_blocks, live_count, False
    )
    col_part = tile_pass(
        local_tiles, local_rows, local_cols, slab, segment_blocks, live_count, True
    )
    summed_rows = reduce_slab(row_part)
    summed_cols = reduce_segment(col_part)
    result = summed_rows + summed_cols + energies[None, :] * vectors.astype(jnp.float32)
    return result.astype(jnp.bfloat16)


def solution(mesh):
    placed = (
        P(None, ("col", "row")),
        P(("col", "row")),
        P("row", "col", None, None, None),
        P("row", "col", None),
        P("row", "col", None),
        P("row", "col"),
    )
    return jax.shard_map(
        body, mesh=mesh, in_specs=placed, out_specs=P(None, ("col", "row")), check_vma=False
    )
```

profile of v0, /device:TPU:1, one launch (start us, length us, event | category | flops | bytes accessed | tf_op | source)
XLA Modules:
  0.0 255.4 jit_solution(633535108928062944)
XLA Ops:
  6.5 0.0 copy-start.2
  6.5 0.0 copy-start.3
  6.5 0.0 reduce-scatter.5.cloned.1.call-start
  7.2 39.5 %all_gather.7 = bf16[8,16384]{1,0:T(8,128)(2,1)S(1)} all-gather(bf16[8,512]{1,0:T(8,128)(2,1)} %param.6), channel_id=1, replica_groups=mesh['row'=8,'col'=32] {'col'}, dimensions={1}, use_global_device_ids=true | all-gather | bytes 270336 | tf_op jit(solution)/shard_map/all_gather | solution.py:41
  46.8 0.7 compare_select_fusion
  47.5 0.8 gather_fusion.1
  48.3 4.7 %fusion.7 = f32[256,8,128]{2,1,0:T(8,128)S(1)} fusion(bf16[256,8,128]{2,1,0:T(8,128)(2,1)S(1)} %gather_fusion.1, bf16[1,1,256,128,128]{4,3,2,1,0:T(8,128)(2,1)} %param.8, pred[256]{0:T(512)(128)(4,1)S(1)} %iota_compare_fusion), kind=kOutput, calls=%fused_computation.9 | convolution fusion | flops 67371008 | bytes 9961728 | tf_op jit(solution)/shard_map/tij,tvi->tvj/dot_general | solution.py:19
  53.0 0.0 copy-start.4
  53.0 0.0 copy-done.3
  53.0 8.4 %scatter_fusion.1 = f32[32,8,128]{2,1,0:T(8,128)S(1)} fusion(f32[32,8,128]{2,1,0:T(8,128)S(1)} %broadcast_in_dim.30, s32[256]{0:T(256)S(1)} %bitcast.37, f32[256,8,128]{2,1,0:T(8,128)S(1)} %fusion.7), kind=kCustom, calls=%fused_computation.3 | custom fusion | flops 262144 | bytes 3146752 | tf_op jit(solution)/shard_map/scatter-add | solution.py:28
  61.4 0.0 copy-start
  61.4 0.0 copy-start.5
  61.5 0.6 copy-done
  62.1 0.0 reduce-scatter.5.cloned.1.call-update
  62.1 0.0 reduce-scatter.3.cloned.1.call-start
  62.2 0.0 copy-done.2
  62.2 28.2 %all_gather.6 = bf16[8,4096]{1,0:T(8,128)(2,1)S(1)} all-gather(bf16[8,512]{1,0:T(8,128)(2,1)S(1)} %copy-done.2), channel_id=1, replica_groups=mesh['row'=8,'col'=32] {'row'}, dimensions={1}, use_global_device_ids=true | all-gather | bytes 73728 | tf_op jit(solution)/shard_map/all_gather | solution.py:52
  90.4 0.8 gather_fusion
  91.2 6.7 %fusion.4 = f32[256,8,128]{2,1,0:T(8,128)S(1)} fusion(bf16[256,8,128]{2,1,0:T(8,128)(2,1)S(1)} %gather_fusion, bf16[1,1,256,128,128]{4,3,2,1,0:T(8,128)(2,1)} %param.8, pred[256]{0:T(512)(128)(4,1)S(1)} %iota_compare_fusion), kind=kOutput, calls=%fused_computation.8 | convolution fusion | flops 67371008 | bytes 9961728 | tf_op jit(solution)/shard_map/tij,tvj->tvi/dot_general | solution.py:22
  98.0 0.1 broadcast_in_dim.27
  98.1 0.0 copy-done.4
  98.1 8.6 %scatter_fusion = f32[128,8,128]{2,1,0:T(8,128)S(1)} fusion(f32[128,8,128]{2,1,0:T(8,128)S(1)} %broadcast_in_dim.27, s32[256]{0:T(256)S(1)} %bitcast.38, f32[256,8,128]{2,1,0:T(8,128)S(1)} %fusion.4), kind=kCustom, calls=%fused_computation.2 | custom fusion | flops 262144 | bytes 3146752 | tf_op jit(solution)/shard_map/scatter-add | solution.py:28
  106.7 0.0 copy-start.1
  106.7 0.8 copy-done.1
  107.5 0.0 reduce-scatter.3.cloned.1.call-update
  107.5 24.1 %reduce-scatter.5.cloned.1.call-done = f32[8,512]{1,0:T(8,128)} async-done(((f32[8,4096]{1,0:T(8,128)}), f32[8,512]{1,0:T(8,128)}) %reduce-scatter.5.cloned.1.call-update) | async-done | bytes 16400 | tf_op jit(solution)/shard_map/reduce_scatter | solution.py:37
  131.6 115.6 %reduce-scatter.3.cloned.1.call-done = f32[8,512]{1,0:T(8,128)} async-done(((f32[8,16384]{1,0:T(8,128)}), f32[8,512]{1,0:T(8,128)}) %reduce-scatter.3.cloned.1.call-update) | async-done | bytes 16400 | tf_op jit(solution)/shard_map/reduce_scatter | solution.py:33
  247.2 0.0 copy-done.5
  247.2 1.3 add_convert_fusion
  (5 shorter events, 0.0 us)
Async XLA Ops:
  6.5 55.6 %copy-start.2 = (bf16[8,512]{1,0:T(8,128)(2,1)S(1)}, bf16[8,512]{1,0:T(8,128)(2,1)}, u32[]{:S(2)}) copy-start(bf16[8,512]{1,0:T(8,128)(2,1)} %param.6) | copy-start | bytes 24580
  6.5 46.4 %copy-start.3 = (s32[1,1,256]{2,1,0:T(1,128)S(1)}, s32[1,1,256]{2,1,0:T(1,128)}, u32[]{:S(2)}) copy-start(s32[1,1,256]{2,1,0:T(1,128)} %param.10) | copy-start | bytes 3076
  6.5 125.1 %reduce-scatter.5.cloned.1.call-start = ((), (), s32[]{:S(2)}) async-start(), calls=%async_computation.3 | async-start | bytes 147456 | tf_op jit(solution)/shard_map/reduce_scatter | solution.py:37
  53.0 45.1 %copy-start.4 = (s32[1,1,256]{2,1,0:T(1,128)S(1)}, s32[1,1,256]{2,1,0:T(1,128)}, u32[]{:S(2)}) copy-start(s32[1,1,256]{2,1,0:T(1,128)} %param.9) | copy-start | bytes 3076
  61.4 0.7 copy-start
  61.4 185.8 %copy-start.5 = (f32[512]{0:T(512)S(1)}, f32[512]{0:T(512)}, u32[]{:S(2)}) copy-start(f32[512]{0:T(512)} %param.7) | copy-start | bytes 6148
  62.1 185.1 %reduce-scatter.3.cloned.1.call-start = ((), (), s32[]{:S(2)}) async-start(), calls=%async_computation.2 | async-start | bytes 540672 | tf_op jit(solution)/shard_map/reduce_scatter | solution.py:33
  106.7 0.8 copy-start.1
Sparse Core Ops, SparseCore 0:
  62.2 69.3 reduce-scatter.4
  134.1 113.0 reduce-scatter.2
where the time goes:
time: 258 us; the launch traced here: 255 us
  waiting for transfers between devices  140 us (54%)
  blocking collectives  67.8 us (26%)
  other arithmetic  19.1 us (7%)
  between operations  14.2 us (6%)
  matrix products  11.4 us (4%)
  local copies, waits for them, and re-layouts  3.13 us (1%)
    reduce_scatter x1, waiting for transfers between devices, reduce_slab(): return lax.psum_scatter(flat_part, 'col', scatter_dimension=1, tiled=True)  116 us
    all_gather x1, blocking collectives, fetch_slab(): return lax.all_gather(vectors, 'col', axis=1, tiled=True)  39.5 us
    all_gather x1, blocking collectives, body(): lax.all_gather(vectors, 'row', axis=1, tiled=True)  28.2 us
    reduce_scatter x1, waiting for transfers between devices, reduce_segment(): lax.psum_scatter(as_flat(col_part), 'row', scatter_dimension=1, tiled=True)  24.1 us
    scatter-add x2, other arithmetic, tile_pass(): return jax.ops.segment_sum(terms, target_index, nseg)  17.1 us
    dot_general x1, matrix products, apply(): jnp.einsum('tij,tvj->tvi', block_tiles, picked, preferred_element_type=jn...  6.74 us
  transfers between devices with their start and end apart: 2, of which 2 were waited for; matrix products, arithmetic and copies ran while one was open for 6% of the time, Pallas kernels for 0%

commit v1 on v0

v1 whole, which is shorter than its diff:
```python
import functools

import jax
import jax.numpy as jnp
from jax import lax
from jax.experimental import pallas as pl
from jax.experimental.pallas import tpu as pltpu
from jax.sharding import PartitionSpec as P

MESH = pl.DeviceIdType.MESH
NT = (((1,), (1,)), ((), ()))
NN = (((1,), (0,)), ((), ()))
BF, F32 = jnp.bfloat16, jnp.float32
LEVEL = 9
GROUP = 32


def remote(src, dst, send, recv, row, col):
    return pltpu.make_async_remote_copy(
        src_ref=src, dst_ref=dst, send_sem=send, recv_sem=recv,
        device_id=(row, col), device_id_type=MESH,
    )


def loop(lo, hi, step):
    lax.fori_loop(lo, hi, lambda i, c: (step(i), c)[1], 0)


def two_terms(x0, x1, t0, t1, forward):
    zero = jnp.zeros_like(x0)
    left = jnp.concatenate([x0, zero], 0).astype(BF)
    right = jnp.concatenate([zero, x1], 0).astype(BF)
    both = jnp.concatenate([left, right], 1)
    pair = jnp.concatenate([t0, t1], 1 if forward else 0)
    return lax.dot_general(both, pair, NT if forward else NN, preferred_element_type=F32)


def collect(picks, terms, slots, nvec, width, store):
    for v in range(nvec):
        term = terms[pl.ds(v, slots, stride=nvec), :]
        high = term.astype(BF)
        low = (term - high.astype(F32)).astype(BF)
        out = jnp.dot(picks, jnp.concatenate([high, low], 1), preferred_element_type=F32)
        store(v, out[:, :width] + out[:, width:])


def kernel(
    nrow, ncol,
    vec, en, tiles, rows, cols, cnt, out,
    tv, vbuf, ebuf, rows_s, rows_v, cols_s, cols_v, cnt_s,
    seg, segf, slab, slabf, terms, mine, other, partner, rsum, csum, crecv,
    tile_sem, in_sem, seg_send, seg_recv, slab_send, slab_recv,
    pair_send, pair_recv, rs_send, rs_recv, cs_send, cs_recv,
):
    slots, width = tv.shape[0], tv.shape[2]
    nvec = vec.shape[0]
    sub = vec.shape[1] // width
    nchip = ncol // 2
    r, c = lax.axis_index("row"), lax.axis_index("col")
    chip, core = c // 2, c % 2

    def chip_at(d):
        return lax.rem(chip + d, nchip)

    def row_at(d):
        return lax.rem(r + d, nrow)

    nch = slots // GROUP
    def tile_copy(g):
        part = pl.ds(pl.multiple_of(g * GROUP, GROUP), GROUP)
        return pltpu.make_async_copy(tiles.at[0, 0, part], tv.at[part], tile_sem.at[g])
    small = [
        pltpu.make_async_copy(s, d, in_sem.at[k])
        for k, (s, d) in enumerate((
            (vec, vbuf), (cols.at[0], cols_s), (rows.at[0], rows_s),
            (cols.at[0], cols_v), (rows.at[0], rows_v), (cnt, cnt_s), (en, ebuf),
        ))
    ]
    for copy in small:
        copy.start()
    loop(0, nch, lambda g: tile_copy(g).start())

    barrier = pltpu.get_barrier_semaphore()
    def greet(row, col):
        pl.semaphore_signal(barrier, inc=1, device_id=(row, col), device_id_type=MESH)
    greet(r, chip * 2 + 1 - core)
    loop(1, nrow, lambda d: greet(row_at(d), c))
    loop(1, nchip, lambda d: greet(r, chip_at(d) * 2 + core))

    for copy in small:
        copy.wait()
    own = jnp.concatenate(
        [vbuf[:, s * width:(s + 1) * width].astype(F32) for s in range(sub)], 0
    )
    seg[r] = own.astype(BF)
    slab[core, chip] = own.astype(BF)
    pl.semaphore_wait(barrier, nrow + nchip - 1)

    def seg_copy(d):
        return remote(seg.at[r], seg.at[r], seg_send.at[d], seg_recv.at[d], row_at(d), c)
    def slab_copy(d):
        return remote(slab.at[core, chip], slab.at[core, chip], slab_send.at[d], slab_recv.at[d],
                      r, chip_at(d) * 2 + core)
    if LEVEL >= 2:
        loop(1, nrow, lambda d: seg_copy(d).start())
        loop(1, nchip, lambda d: slab_copy(d).start())

    live = lax.broadcasted_iota(jnp.int32, (1, slots), 1) < cnt_s[0, 0]
    a, b = rows_v[...], cols_v[...]
    place = (a // sub % 2) * (nchip * sub) + (a // (2 * sub)) * sub + a % sub
    place = jnp.where(live, place, -1)
    b = jnp.where(live, b, -1)

    def picks(targets, first, count):
        index = lax.broadcasted_iota(jnp.int32, (count, slots), 0) + first
        return (index == targets).astype(BF)

    pair_slab = remote(slab.at[core], slab.at[core], pair_send.at[0], pair_recv.at[0],
                       r, chip * 2 + 1 - core)
    pair_sum = remote(other, partner, pair_send.at[1], pair_recv.at[1], r, chip * 2 + 1 - core)
    nb = nrow * sub

    if LEVEL >= 2:
        loop(1, nrow, lambda d: seg_copy(d).wait_recv())
        for k in range(nrow):
            block = seg[k].astype(F32)
            for s in range(sub):
                segf[k * sub + s] = block[s * nvec:(s + 1) * nvec]

    def forward(g):
        tile_copy(g).wait()
        for u in range(0, GROUP, 2):
            t = g * GROUP + u
            terms[pl.ds(pl.multiple_of(t * nvec, 2 * nvec), 2 * nvec), :] = two_terms(
                segf[cols_s[0, t]], segf[cols_s[0, t + 1]], tv[t], tv[t + 1], True)
        @pl.when(g == nch // 2)
        def _():
            loop(1, nchip, lambda d: slab_copy(d).wait_recv())
            pair_slab.start()

    def backward(g):
        for u in range(0, GROUP, 2):
            t = g * GROUP + u
            terms[pl.ds(pl.multiple_of(t * nvec, 2 * nvec), 2 * nvec), :] = two_terms(
                slabf[rows_s[0, t]], slabf[rows_s[0, t + 1]], tv[t], tv[t + 1], False)

    half = nchip * sub
    if LEVEL >= 3:
        loop(0, nch, forward)
    if LEVEL >= 4:
        def keep(ref):
            def store(v, x):
                ref[pl.ds(v, half, stride=nvec), :] = x
            return store
        collect(picks(place, (1 - core) * half, half), terms, slots, nvec, width, keep(other))
        pair_sum.start()
        collect(picks(place, core * half, half), terms, slots, nvec, width, keep(mine))

    size = sub * nvec
    def rs_copy(d):
        there = pl.ds(pl.multiple_of(chip_at(d) * size, size), size)
        return remote(mine.at[there], rsum.at[d], rs_send.at[d], rs_recv.at[d],
                      r, chip_at(d) * 2 + core)
    if LEVEL >= 5:
        pair_slab.wait_recv()
        for k in range(nchip):
            for m in range(2):
                block = slab[m, k].astype(F32)
                for s in range(sub):
                    slabf[(k * 2 + m) * sub + s] = block[s * nvec:(s + 1) * nvec]
        loop(0, nch // 4, backward)
        pair_sum.wait_recv()
        mine[...] += partner[...]
        loop(1, nchip, lambda d: rs_copy(d).start())
    if LEVEL >= 6:
        loop(nch // 4, nch, backward)
        def keep_cols(v, x):
            csum[pl.ds(v, nb, stride=nvec), :] = x
        collect(picks(b, 0, nb), terms, slots, nvec, width, keep_cols)
    def cs_copy(d):
        there = pl.ds(pl.multiple_of(row_at(d) * size, size), size)
        return remote(csum.at[there], crecv.at[d], cs_send.at[d], cs_recv.at[d], row_at(d), c)
    if LEVEL >= 7:
        loop(1, nrow, lambda d: cs_copy(d).start())

    total = own
    if LEVEL >= 6:
        total = jnp.concatenate(
            [own[s * nvec:(s + 1) * nvec] * ebuf[:, s * width:(s + 1) * width] for s in range(sub)], 0)
    if LEVEL >= 5:
        total = total + mine[pl.ds(pl.multiple_of(chip * size, size), size), :]
        loop(1, nchip, lambda d: rs_copy(d).wait_recv())
        for d in range(1, nchip):
            total = total + rsum[d]
    if LEVEL >= 7:
        total = total + csum[pl.ds(pl.multiple_of(r * size, size), size), :]
        loop(1, nrow, lambda d: cs_copy(d).wait_recv())
        for d in range(1, nrow):
            total = total + crecv[d]
    for s in range(sub):
        out[:, s * width:(s + 1) * width] = total[s * nvec:(s + 1) * nvec].astype(BF)

    if LEVEL >= 2:
        loop(1, nrow, lambda d: seg_copy(d).wait_send())
        loop(1, nchip, lambda d: slab_copy(d).wait_send())
    if LEVEL == 2:
        loop(1, nchip, lambda d: slab_copy(d).wait_recv())
    if LEVEL < 3:
        loop(0, nch, lambda g: tile_copy(g).wait())
    if LEVEL >= 3:
        pair_slab.wait_send()
        if LEVEL < 5:
            pair_slab.wait_recv()
    if LEVEL >= 4:
        pair_sum.wait_send()
        if LEVEL < 5:
            pair_sum.wait_recv()
    if LEVEL >= 5:
        loop(1, nchip, lambda d: rs_copy(d).wait_send())
    if LEVEL >= 7:
        loop(1, nrow, lambda d: cs_copy(d).wait_send())


def body(vectors, energies, tiles, tile_rows, tile_cols, counts):
    nrow, ncol = lax.axis_size("row"), lax.axis_size("col")
    slots, width = tiles.shape[2], tiles.shape[3]
    nvec, own = vectors.shape
    sub = own // width
    nchip = ncol // 2
    any_, dma = pl.BlockSpec(memory_space=pl.ANY), pltpu.SemaphoreType.DMA
    return pl.pallas_call(
        functools.partial(kernel, nrow, ncol),
        out_shape=jax.ShapeDtypeStruct(vectors.shape, BF),
        in_specs=[any_] * 6,
        out_specs=pl.BlockSpec(memory_space=pltpu.VMEM),
        scratch_shapes=[
            pltpu.VMEM((slots, width, width), BF),
            pltpu.VMEM((nvec, own), BF),
            pltpu.VMEM((1, own), F32),
            pltpu.SMEM((1, slots), jnp.int32),
            pltpu.VMEM((1, slots), jnp.int32),
            pltpu.SMEM((1, slots), jnp.int32),
            pltpu.VMEM((1, slots), jnp.int32),
            pltpu.SMEM((1, 1), jnp.int32),
            pltpu.VMEM((nrow, sub * nvec, width), BF),
            pltpu.VMEM((nrow * sub, nvec, width), F32),
            pltpu.VMEM((2, nchip, sub * nvec, width), BF),
            pltpu.VMEM((ncol * sub, nvec, width), F32),
            pltpu.VMEM((slots * nvec, width), F32),
            pltpu.VMEM((nchip * sub * nvec, width), F32),
            pltpu.VMEM((nchip * sub * nvec, width), F32),
            pltpu.VMEM((nchip * sub * nvec, width), F32),
            pltpu.VMEM((nchip, sub * nvec, width), F32),
            pltpu.VMEM((nrow * sub * nvec, width), F32),
            pltpu.VMEM((nrow, sub * nvec, width), F32),
            dma((slots // GROUP,)), dma((7,)),
            dma((nrow,)), dma((nrow,)), dma((nchip,)), dma((nchip,)),
            dma((2,)), dma((2,)), dma((nchip,)), dma((nchip,)), dma((nrow,)), dma((nrow,)),
        ],
        compiler_params=pltpu.CompilerParams(
            collective_id=0, has_side_effects=True, vmem_limit_bytes=56 * 2**20
        ),
    )(vectors, energies.reshape(1, own), tiles, tile_rows, tile_cols, counts)


def solution(mesh):
    placed = (
        P(None, ("col", "row")),
        P(("col", "row")),
        P("row", "col", None, None, None),
        P("row", "col", None),
        P("row", "col", None),
        P("row", "col"),
    )
    return jax.shard_map(
        body, mesh=mesh, in_specs=placed, out_specs=P(None, ("col", "row")), check_vma=False
    )
```

time: 258 us -> 33.4 us (0.13)
  waiting for transfers between devices: 140 us -> 0 us
  blocking collectives: 67.8 us -> 0 us
  Pallas kernels: 0 us -> 31.3 us
  other arithmetic: 19.1 us -> 0 us
  between operations: 14.2 us -> 0.66 us
  matrix products: 11.4 us -> 0 us
    reduce_scatter x2 -> x0, waiting for transfers between devices: 140 us -> none  [the longest x1 116 us: reduce_slab(): return lax.psum_scatter(flat_part, 'col', scatter_dimension=1, tiled=True)]
    all_gather x2 -> x0, blocking collectives: 67.8 us -> none  [the longest x1 39.5 us: fetch_slab(): return lax.all_gather(vectors, 'col', axis=1, tiled=True)]
    pallas_call x0 -> x1, Pallas kernels: none -> 31.3 us  [body(): pl.pallas_call(functools.partial(kernel, nrow, ncol), out_shape=jax.Shape...]
    scatter-add x2 -> x0, other arithmetic: 17.1 us -> none  [tile_pass(): return jax.ops.segment_sum(terms, target_index, nseg)]
    dot_general x2 -> x0, matrix products: 11.4 us -> none  [the longest x1 6.74 us: apply(): jnp.einsum('tij,tvj->tvi', block_tiles, picked, preferred_element_type=jn...]
  transfers between devices with their start and end apart: 2 -> 0, of which waited for: 2 -> 0; matrix products, arithmetic and copies ran while one was open for 6% -> 0% of each run, Pallas kernels for 0% -> 0%
where the time goes in v1:
time: 33.4 us; the launch traced here: 33.2 us
  Pallas kernels  31.3 us (94%)
  local copies, waits for them, and re-layouts  1.3 us (4%)
  between operations  0.66 us (2%)
    pallas_call x1, Pallas kernels, body(): pl.pallas_call(functools.partial(kernel, nrow, ncol), out_shape=jax.Shape...  31.3 us
    unnamed x1, local copies, waits for them, and re-layouts  1.3 us

profile of v1, /device:TPU:1, one launch (start us, length us, event | category | flops | bytes accessed | tf_op | source)
XLA Modules:
  0.0 33.2 jit_solution(7796998988706941838)
XLA Ops:
  0.7 31.3 %shard_map.64 = bf16[8,512]{1,0:T(8,128)(2,1)} custom-call(bf16[8,512]{1,0:T(8,128)(2,1)} %vec.1, f32[1,512]{1,0:T(1,128)} %bitcast.1, bf16[1,1,256,128,128]{4,3,2,1,0:T(8,128)(2,1)} %tiles.1, s32[1,1,256]{2,1,0:T(1,128)} %rows.1, s32[1,1,256]{2,1,0:T(1,128)} %cols.1, s32[1,1]{1,0:T(1,128)S(6)} %copy.8.cnt), custom_call_target="tpu_custom_call" | custom-call | tf_op jit(solution)/shard_map/pallas_call | solution.py:231
  31.9 1.3 %copy.9 = bf16[8,512]{1,0:T(8,128)(2,1)} copy(bf16[8,512]{1,0:T(8,128)(2,1)} %shard_map.64) | data formatting | bytes 16384

commit v2 on v1

v2 whole, which is shorter than its diff:
```python
import functools

import jax
import jax.numpy as jnp
from jax import lax
from jax.experimental import pallas as pl
from jax.experimental.pallas import tpu as pltpu
from jax.sharding import PartitionSpec as P

MESH = pl.DeviceIdType.MESH
NT = (((1,), (1,)), ((), ()))
NN = (((1,), (0,)), ((), ()))
BF, F32 = jnp.bfloat16, jnp.float32
GROUP = 128
PIECES = 4


def remote(src, dst, send, recv, row, col):
    return pltpu.make_async_remote_copy(
        src_ref=src, dst_ref=dst, send_sem=send, recv_sem=recv,
        device_id=(row, col), device_id_type=MESH,
    )


def loop(lo, hi, step):
    lax.fori_loop(lo, hi, lambda i, c: (step(i), c)[1], 0)


def two_terms(x0, x1, t0, t1, forward):
    zero = jnp.zeros_like(x0)
    left = jnp.concatenate([x0, zero], 0).astype(BF)
    right = jnp.concatenate([zero, x1], 0).astype(BF)
    both = jnp.concatenate([left, right], 1)
    pair = jnp.concatenate([t0, t1], 1 if forward else 0)
    return lax.dot_general(both, pair, NT if forward else NN, preferred_element_type=F32)


def collect(picks, terms, slots, nvec, width, store):
    for v in range(nvec):
        term = terms[pl.ds(v, slots, stride=nvec), :]
        high = term.astype(BF)
        low = (term - high.astype(F32)).astype(BF)
        out = jnp.dot(picks, jnp.concatenate([high, low], 1), preferred_element_type=F32)
        store(v, out[:, :width] + out[:, width:])


def kernel(
    nrow, ncol,
    vec, en, tiles, rows, cols, cnt, out,
    tv, vbuf, ebuf, rows_s, rows_v, cols_s, cols_v, cnt_s,
    seg, segf, slab, slabf, terms, mine, other, partner, rsum, csum, crecv,
    tile_sem, in_sem, seg_send, seg_recv, slab_send, slab_recv,
    pair_send, pair_recv, rs_send, rs_recv, cs_send, cs_recv, ready,
):
    slots, width = tv.shape[0], tv.shape[2]
    nvec = vec.shape[0]
    sub = vec.shape[1] // width
    nchip = ncol // 2
    r, c = lax.axis_index("row"), lax.axis_index("col")
    chip, core = c // 2, c % 2

    def row_at(d):
        return lax.rem(r + d, nrow)

    split = nchip // 2
    barrier = pltpu.get_barrier_semaphore()
    def greet(row, col):
        pl.semaphore_signal(barrier, inc=1, device_id=(row, col), device_id_type=MESH)
    greet(r, chip * 2 + 1 - core)
    loop(1, nrow, lambda d: greet(row_at(d), c))
    loop(chip + 1, nchip, lambda k: greet(r, k * 2 + core))
    @pl.when(chip < split)
    def _():
        loop(0, chip, lambda k: greet(r, k * 2 + core))

    nch = slots // GROUP
    def tile_copy(g):
        part = pl.ds(pl.multiple_of(g * GROUP, GROUP), GROUP)
        return pltpu.make_async_copy(tiles.at[0, 0, part], tv.at[part], tile_sem.at[g])
    small = [
        pltpu.make_async_copy(s, d, in_sem.at[k])
        for k, (s, d) in enumerate((
            (vec, vbuf), (cols.at[0], cols_s), (rows.at[0], rows_s),
            (cols.at[0], cols_v), (rows.at[0], rows_v), (cnt, cnt_s), (en, ebuf),
        ))
    ]
    for copy in small:
        copy.start()
    loop(0, nch, lambda g: tile_copy(g).start())

    for copy in small:
        copy.wait()
    own = jnp.concatenate(
        [vbuf[:, s * width:(s + 1) * width].astype(F32) for s in range(sub)], 0
    )
    seg[r] = own.astype(BF)
    slab[core, chip] = own.astype(BF)

    live = lax.broadcasted_iota(jnp.int32, (1, slots), 1) < cnt_s[0, 0]
    a, b = rows_v[...], cols_v[...]
    place = (a // sub % 2) * (nchip * sub) + (a // (2 * sub)) * sub + a % sub
    place = jnp.where(live, place, -1)
    b = jnp.where(live, b, -1)

    def picks(targets, first, count):
        index = lax.broadcasted_iota(jnp.int32, (count, slots), 0) + first
        return (index == targets).astype(BF)

    near = chip < split
    pl.semaphore_wait(barrier, nrow + jnp.where(near, split - 1, chip))

    def seg_copy(d):
        return remote(seg.at[r], seg.at[r], seg_send.at[d], seg_recv.at[d], row_at(d), c)
    def slab_out(k):
        return remote(slab.at[core, chip], slab.at[core, chip], slab_send.at[k], slab_recv.at[chip],
                      r, k * 2 + core)
    def slab_in(k):
        return remote(slab.at[core, k], slab.at[core, k], slab_send.at[k], slab_recv.at[k],
                      r, k * 2 + core)
    loop(1, nrow, lambda d: seg_copy(d).start())
    first_far = jnp.maximum(chip + 1, split)
    loop(chip + 1, split, lambda k: slab_out(k).start())
    @pl.when(jnp.logical_not(near))
    def _():
        loop(0, chip, lambda k: pl.semaphore_signal(
            ready.at[chip], inc=1, device_id=(r, k * 2 + core), device_id_type=MESH))

    pair_slab = remote(slab.at[core], slab.at[core], pair_send.at[0], pair_recv.at[0],
                       r, chip * 2 + 1 - core)
    nb = nrow * sub
    size = sub * nvec
    piece = nchip // PIECES

    loop(1, nrow, lambda d: seg_copy(d).wait_recv())
    for k in range(nrow):
        block = seg[k].astype(F32)
        for s in range(sub):
            segf[k * sub + s] = block[s * nvec:(s + 1) * nvec]

    def relay():
        loop(0, chip, lambda k: slab_in(k).wait_recv())
        pair_slab.start()

    def to_far(k):
        pl.semaphore_wait(ready.at[k], 1)
        slab_out(k).start()

    def forward(g):
        @pl.when(g == nch // 2)
        def _():
            pl.when(near)(relay)
            loop(first_far, nchip, to_far)
        tile_copy(g).wait()
        for u in range(0, GROUP, 2):
            t = g * GROUP + u
            terms[pl.ds(pl.multiple_of(t * nvec, 2 * nvec), 2 * nvec), :] = two_terms(
                segf[cols_s[0, t]], segf[cols_s[0, t + 1]], tv[t], tv[t + 1], True)

    loop(0, nch, forward)

    half = nchip * sub
    def keep(ref):
        def store(v, x):
            ref[pl.ds(v, half, stride=nvec), :] = x
        return store

    def pair_sum(q):
        part = pl.ds(pl.multiple_of(q * piece * size, piece * size), piece * size)
        return remote(other.at[part], partner.at[part], pair_send.at[1 + q], pair_recv.at[1 + q],
                      r, chip * 2 + 1 - core)
    npiece = chip // piece + 1
    collect(picks(place, (1 - core) * half, half), terms, slots, nvec, width, keep(other))
    loop(0, npiece, lambda q: pair_sum(q).start())
    collect(picks(place, core * half, half), terms, slots, nvec, width, keep(mine))

    def rs_out(k):
        there = pl.ds(pl.multiple_of(k * size, size), size)
        return remote(mine.at[there], rsum.at[chip], rs_send.at[k], rs_recv.at[chip], r, k * 2 + core)
    def rs_in(k):
        return remote(rsum.at[k], rsum.at[k], rs_send.at[k], rs_recv.at[k], r, k * 2 + core)

    def send_rows():
        def one(q):
            pair_sum(q).wait_recv()
            part = pl.ds(pl.multiple_of(q * piece * size, piece * size), piece * size)
            mine[part, :] += partner[part, :]
            loop(q * piece, jnp.minimum((q + 1) * piece, chip), lambda k: rs_out(k).start())
        loop(0, npiece, one)

    @pl.when(jnp.logical_not(near))
    def _():
        send_rows()
        relay()

    pair_slab.wait_recv()
    for k in range(nchip):
        for m in range(2):
            block = slab[m, k].astype(F32)
            for s in range(sub):
                slabf[(k * 2 + m) * sub + s] = block[s * nvec:(s + 1) * nvec]

    def backward(g):
        @pl.when(jnp.logical_and(near, g == nch // 2))
        def _():
            send_rows()
        for u in range(0, GROUP, 2):
            t = g * GROUP + u
            terms[pl.ds(pl.multiple_of(t * nvec, 2 * nvec), 2 * nvec), :] = two_terms(
                slabf[rows_s[0, t]], slabf[rows_s[0, t + 1]], tv[t], tv[t + 1], False)

    loop(0, nch, backward)
    def keep_cols(v, x):
        csum[pl.ds(v, nb, stride=nvec), :] = x
    collect(picks(b, 0, nb), terms, slots, nvec, width, keep_cols)
    def cs_copy(d):
        there = pl.ds(pl.multiple_of(row_at(d) * size, size), size)
        return remote(csum.at[there], crecv.at[d], cs_send.at[d], cs_recv.at[d], row_at(d), c)
    loop(1, nrow, lambda d: cs_copy(d).start())

    total = jnp.concatenate(
        [own[s * nvec:(s + 1) * nvec] * ebuf[:, s * width:(s + 1) * width] for s in range(sub)], 0)
    total = total + mine[pl.ds(pl.multiple_of(chip * size, size), size), :]
    total = total + csum[pl.ds(pl.multiple_of(r * size, size), size), :]
    def add_cols(d, x):
        cs_copy(d).wait_recv()
        return x + crecv[d]
    def add_rows(k, x):
        rs_in(k).wait_recv()
        return x + rsum[k]
    total = lax.fori_loop(1, nrow, add_cols, total)
    total = lax.fori_loop(chip + 1, nchip, add_rows, total)
    for s in range(sub):
        out[:, s * width:(s + 1) * width] = total[s * nvec:(s + 1) * nvec].astype(BF)

    loop(1, nrow, lambda d: seg_copy(d).wait_send())
    loop(chip + 1, nchip, lambda k: slab_out(k).wait_send())
    pair_slab.wait_send()
    loop(0, npiece, lambda q: pair_sum(q).wait_send())
    loop(0, chip, lambda k: rs_out(k).wait_send())
    loop(1, nrow, lambda d: cs_copy(d).wait_send())


def body(vectors, energies, tiles, tile_rows, tile_cols, counts):
    nrow, ncol = lax.axis_size("row"), lax.axis_size("col")
    slots, width = tiles.shape[2], tiles.shape[3]
    nvec, own = vectors.shape
    sub = own // width
    nchip = ncol // 2
    any_, dma = pl.BlockSpec(memory_space=pl.ANY), pltpu.SemaphoreType.DMA
    return pl.pallas_call(
        functools.partial(kernel, nrow, ncol),
        out_shape=pltpu.VMEM(vectors.shape, BF),
        in_specs=[any_] * 6,
        out_specs=pl.BlockSpec(memory_space=pltpu.VMEM),
        scratch_shapes=[
            pltpu.VMEM((slots, width, width), BF),
            pltpu.VMEM((nvec, own), BF),
            pltpu.VMEM((1, own), F32),
            pltpu.SMEM((1, slots), jnp.int32),
            pltpu.VMEM((1, slots), jnp.int32),
            pltpu.SMEM((1, slots), jnp.int32),
            pltpu.VMEM((1, slots), jnp.int32),
            pltpu.SMEM((1, 1), jnp.int32),
            pltpu.VMEM((nrow, sub * nvec, width), BF),
            pltpu.VMEM((nrow * sub, nvec, width), F32),
            pltpu.VMEM((2, nchip, sub * nvec, width), BF),
            pltpu.VMEM((ncol * sub, nvec, width), F32),
            pltpu.VMEM((slots * nvec, width), F32),
            pltpu.VMEM((nchip * sub * nvec, width), F32),
            pltpu.VMEM((nchip * sub * nvec, width), F32),
            pltpu.VMEM((nchip * sub * nvec, width), F32),
            pltpu.VMEM((nchip, sub * nvec, width), F32),
            pltpu.VMEM((nrow * sub * nvec, width), F32),
            pltpu.VMEM((nrow, sub * nvec, width), F32),
            dma((slots // GROUP,)), dma((7,)),
            dma((nrow,)), dma((nrow,)), dma((nchip,)), dma((nchip,)),
            dma((1 + PIECES,)), dma((1 + PIECES,)), dma((nchip,)), dma((nchip,)), dma((nrow,)), dma((nrow,)),
            pltpu.SemaphoreType.REGULAR((nchip,)),
        ],
        compiler_params=pltpu.CompilerParams(
            collective_id=0, has_side_effects=True, vmem_limit_bytes=56 * 2**20
        ),
    )(vectors, energies.reshape(1, own), tiles, tile_rows, tile_cols, counts)


def solution(mesh):
    placed = (
        P(None, ("col", "row")),
        P(("col", "row")),
        P("row", "col", None, None, None),
        P("row", "col", None),
        P("row", "col", None),
        P("row", "col"),
    )
    return jax.shard_map(
        body, mesh=mesh, in_specs=placed, out_specs=P(None, ("col", "row")), check_vma=False
    )
```

time: 33.4 us -> 28.4 us (0.85)
  Pallas kernels: 31.3 us -> 27 us
  local copies, waits for them, and re-layouts: 1.3 us -> 0.6 us
    pallas_call x1, Pallas kernels: 31.3 us -> 27 us  [body(): pl.pallas_call(functools.partial(kernel, nrow, ncol), out_shape=pltpu.VME...]
    unnamed x1, local copies, waits for them, and re-layouts: 1.3 us -> 0.6 us
where the time goes in v2:
time: 28.4 us; the launch traced here: 28.2 us
  Pallas kernels  27 us (95%)
  between operations  0.66 us (2%)
  local copies, waits for them, and re-layouts  0.6 us (2%)
    pallas_call x1, Pallas kernels, body(): pl.pallas_call(functools.partial(kernel, nrow, ncol), out_shape=pltpu.VME...  27 us
    unnamed x1, local copies, waits for them, and re-layouts  0.6 us

profile of v2, /device:TPU:1, one launch (start us, length us, event | category | flops | bytes accessed | tf_op | source)
XLA Modules:
  0.0 28.2 jit_solution(9568167354243162387)
XLA Ops:
  0.7 27.0 %shard_map.64 = bf16[8,512]{1,0:T(8,128)(2,1)S(1)} custom-call(bf16[8,512]{1,0:T(8,128)(2,1)} %vec.1, f32[1,512]{1,0:T(1,128)} %bitcast.1, bf16[1,1,256,128,128]{4,3,2,1,0:T(8,128)(2,1)} %tiles.1, s32[1,1,256]{2,1,0:T(1,128)} %rows.1, s32[1,1,256]{2,1,0:T(1,128)} %cols.1, s32[1,1]{1,0:T(1,128)S(6)} %copy.9.cnt), custom_call_target="tpu_custom_call" | custom-call | tf_op jit(solution)/shard_map/pallas_call | solution.py:250
  27.6 0.6 %copy.8 = bf16[8,512]{1,0:T(8,128)(2,1)} copy(bf16[8,512]{1,0:T(8,128)(2,1)S(1)} %shard_map.64) | data formatting | bytes 16384

commit v3 on v2

--- a/solution.py
+++ b/solution.py
@@ -8,10 +8,11 @@
 from jax.sharding import PartitionSpec as P
 
 MESH = pl.DeviceIdType.MESH
-NT = (((1,), (1,)), ((), ()))
-NN = (((1,), (0,)), ((), ()))
 BF, F32 = jnp.bfloat16, jnp.float32
 GROUP = 128
+EARLY = 8
+TURN = 32
+LIMIT = 32767.0
 PIECES = 4
 
 
@@ -26,13 +27,12 @@
     lax.fori_loop(lo, hi, lambda i, c: (step(i), c)[1], 0)
 
 
-def two_terms(x0, x1, t0, t1, forward):
+def two_terms(x0, x1, t0, t1):
     zero = jnp.zeros_like(x0)
     left = jnp.concatenate([x0, zero], 0).astype(BF)
     right = jnp.concatenate([zero, x1], 0).astype(BF)
     both = jnp.concatenate([left, right], 1)
-    pair = jnp.concatenate([t0, t1], 1 if forward else 0)
-    return lax.dot_general(both, pair, NT if forward else NN, preferred_element_type=F32)
+    return jnp.dot(both, jnp.concatenate([t0, t1], 0), preferred_element_type=F32)
 
 
 def collect(picks, terms, slots, nvec, width, store):
@@ -47,8 +47,8 @@
 def kernel(
     nrow, ncol,
     vec, en, tiles, rows, cols, cnt, out,
-    tv, vbuf, ebuf, rows_s, rows_v, cols_s, cols_v, cnt_s,
-    seg, segf, slab, slabf, terms, mine, other, partner, rsum, csum, crecv,
+    tv, flip, vbuf, ebuf, rows_s, rows_v, cols_s, cols_v, cnt_s,
+    seg, segf, slab, slabf, terms, mine, other, partner, fixed, scale, rsum, rscale, csum, crecv,
     tile_sem, in_sem, seg_send, seg_recv, slab_send, slab_recv,
     pair_send, pair_recv, rs_send, rs_recv, cs_send, cs_recv, ready,
 ):
@@ -62,20 +62,16 @@
     def row_at(d):
         return lax.rem(r + d, nrow)
 
-    split = nchip // 2
     barrier = pltpu.get_barrier_semaphore()
     def greet(row, col):
         pl.semaphore_signal(barrier, inc=1, device_id=(row, col), device_id_type=MESH)
     greet(r, chip * 2 + 1 - core)
     loop(1, nrow, lambda d: greet(row_at(d), c))
     loop(chip + 1, nchip, lambda k: greet(r, k * 2 + core))
-    @pl.when(chip < split)
-    def _():
-        loop(0, chip, lambda k: greet(r, k * 2 + core))
-
-    nch = slots // GROUP
+
+    nch = slots // TURN
     def tile_copy(g):
-        part = pl.ds(pl.multiple_of(g * GROUP, GROUP), GROUP)
+        part = pl.ds(pl.multiple_of(g * TURN, TURN), TURN)
         return pltpu.make_async_copy(tiles.at[0, 0, part], tv.at[part], tile_sem.at[g])
     small = [
         pltpu.make_async_copy(s, d, in_sem.at[k])
@@ -106,8 +102,7 @@
         index = lax.broadcasted_iota(jnp.int32, (count, slots), 0) + first
         return (index == targets).astype(BF)
 
-    near = chip < split
-    pl.semaphore_wait(barrier, nrow + jnp.where(near, split - 1, chip))
+    pl.semaphore_wait(barrier, nrow + chip)
 
     def seg_copy(d):
         return remote(seg.at[r], seg.at[r], seg_send.at[d], seg_recv.at[d], row_at(d), c)
@@ -118,12 +113,14 @@
         return remote(slab.at[core, k], slab.at[core, k], slab_send.at[k], slab_recv.at[k],
                       r, k * 2 + core)
     loop(1, nrow, lambda d: seg_copy(d).start())
-    first_far = jnp.maximum(chip + 1, split)
-    loop(chip + 1, split, lambda k: slab_out(k).start())
-    @pl.when(jnp.logical_not(near))
-    def _():
-        loop(0, chip, lambda k: pl.semaphore_signal(
-            ready.at[chip], inc=1, device_id=(r, k * 2 + core), device_id_type=MESH))
+    loop(0, chip, lambda k: pl.semaphore_signal(
+        ready.at[chip], inc=1, device_id=(r, k * 2 + core), device_id_type=MESH))
+
+    def turn(g):
+        tile_copy(g).wait()
+        for u in range(TURN):
+            flip[g * TURN + u] = tv[g * TURN + u].T
+    loop(0, nch, turn)
 
     pair_slab = remote(slab.at[core], slab.at[core], pair_send.at[0], pair_recv.at[0],
                        r, chip * 2 + 1 - core)
@@ -141,22 +138,25 @@
         loop(0, chip, lambda k: slab_in(k).wait_recv())
         pair_slab.start()
 
-    def to_far(k):
+    def to_later(k):
         pl.semaphore_wait(ready.at[k], 1)
         slab_out(k).start()
 
-    def forward(g):
-        @pl.when(g == nch // 2)
-        def _():
-            pl.when(near)(relay)
-            loop(first_far, nchip, to_far)
-        tile_copy(g).wait()
-        for u in range(0, GROUP, 2):
-            t = g * GROUP + u
-            terms[pl.ds(pl.multiple_of(t * nvec, 2 * nvec), 2 * nvec), :] = two_terms(
-                segf[cols_s[0, t]], segf[cols_s[0, t + 1]], tv[t], tv[t + 1], True)
-
-    loop(0, nch, forward)
+    def products(source, index, matrix):
+        def step(g):
+            for u in range(0, GROUP, 2):
+                t = g * GROUP + u
+                terms[pl.ds(pl.multiple_of(t * nvec, 2 * nvec), 2 * nvec), :] = two_terms(
+                    source[index[0, t]], source[index[0, t + 1]], matrix[t], matrix[t + 1])
+        loop(0, slots // GROUP, step)
+
+    early = chip < max(nchip // EARLY, 1)
+    first = chip < max(nchip // 8, 1)
+    split = nchip // 2
+    @pl.when(jnp.logical_not(early))
+    def _():
+        loop(chip + 1, nchip, to_later)
+    products(segf, cols_s, flip)
 
     half = nchip * sub
     def keep(ref):
@@ -174,23 +174,40 @@
     collect(picks(place, core * half, half), terms, slots, nvec, width, keep(mine))
 
     def rs_out(k):
-        there = pl.ds(pl.multiple_of(k * size, size), size)
-        return remote(mine.at[there], rsum.at[chip], rs_send.at[k], rs_recv.at[chip], r, k * 2 + core)
+        to = (r, k * 2 + core)
+        return (remote(fixed.at[k], rsum.at[chip], rs_send.at[0, k], rs_recv.at[0, chip], *to),
+                remote(scale.at[k], rscale.at[chip], rs_send.at[1, k], rs_recv.at[1, chip], *to))
     def rs_in(k):
-        return remote(rsum.at[k], rsum.at[k], rs_send.at[k], rs_recv.at[k], r, k * 2 + core)
-
-    def send_rows():
-        def one(q):
-            pair_sum(q).wait_recv()
-            part = pl.ds(pl.multiple_of(q * piece * size, piece * size), piece * size)
-            mine[part, :] += partner[part, :]
-            loop(q * piece, jnp.minimum((q + 1) * piece, chip), lambda k: rs_out(k).start())
-        loop(0, npiece, one)
-
-    @pl.when(jnp.logical_not(near))
+        to = (r, k * 2 + core)
+        return (remote(rsum.at[k], rsum.at[k], rs_send.at[0, k], rs_recv.at[0, k], *to),
+                remote(rscale.at[k], rscale.at[k], rs_send.at[1, k], rs_recv.at[1, k], *to))
+    def rs_start(k):
+        for copy in rs_out(k):
+            copy.start()
+    def rs_wait(k):
+        for copy in rs_out(k):
+            copy.wait_send()
+
+    def send_rows(q):
+        pair_sum(q).wait_recv()
+        for u in range(piece):
+            k = q * piece + u
+            part = pl.ds(pl.multiple_of(k * size, size), size)
+            x = mine[part, :] + partner[part, :]
+            mine[part, :] = x
+            most = jnp.max(jnp.abs(x), axis=0, keepdims=True)
+            some = most > 1e-30
+            fixed[k] = jnp.round(x * jnp.where(some, LIMIT / jnp.where(some, most, 1.0), 0.0)).astype(jnp.int32).astype(jnp.int16)
+            scale[k] = most * (1.0 / LIMIT)
+        loop(q * piece, jnp.minimum((q + 1) * piece, chip), rs_start)
+    loop(0, npiece, send_rows)
+
+    @pl.when(early)
     def _():
-        send_rows()
-        relay()
+        loop(chip + 1, split, to_later)
+        pl.when(first)(relay)
+        loop(split, nchip, to_later)
+    pl.when(jnp.logical_not(first))(relay)
 
     pair_slab.wait_recv()
     for k in range(nchip):
@@ -199,16 +216,7 @@
             for s in range(sub):
                 slabf[(k * 2 + m) * sub + s] = block[s * nvec:(s + 1) * nvec]
 
-    def backward(g):
-        @pl.when(jnp.logical_and(near, g == nch // 2))
-        def _():
-            send_rows()
-        for u in range(0, GROUP, 2):
-            t = g * GROUP + u
-            terms[pl.ds(pl.multiple_of(t * nvec, 2 * nvec), 2 * nvec), :] = two_terms(
-                slabf[rows_s[0, t]], slabf[rows_s[0, t + 1]], tv[t], tv[t + 1], False)
-
-    loop(0, nch, backward)
+    products(slabf, rows_s, tv)
     def keep_cols(v, x):
         csum[pl.ds(v, nb, stride=nvec), :] = x
     collect(picks(b, 0, nb), terms, slots, nvec, width, keep_cols)
@@ -225,8 +233,9 @@
         cs_copy(d).wait_recv()
         return x + crecv[d]
     def add_rows(k, x):
-        rs_in(k).wait_recv()
-        return x + rsum[k]
+        for copy in rs_in(k):
+            copy.wait_recv()
+        return x + rsum[k].astype(jnp.int32).astype(F32) * rscale[k]
     total = lax.fori_loop(1, nrow, add_cols, total)
     total = lax.fori_loop(chip + 1, nchip, add_rows, total)
     for s in range(sub):
@@ -236,7 +245,7 @@
     loop(chip + 1, nchip, lambda k: slab_out(k).wait_send())
     pair_slab.wait_send()
     loop(0, npiece, lambda q: pair_sum(q).wait_send())
-    loop(0, chip, lambda k: rs_out(k).wait_send())
+    loop(0, chip, rs_wait)
     loop(1, nrow, lambda d: cs_copy(d).wait_send())
 
 
@@ -253,6 +262,7 @@
         in_specs=[any_] * 6,
         out_specs=pl.BlockSpec(memory_space=pltpu.VMEM),
         scratch_shapes=[
+            pltpu.VMEM((slots, width, width), BF),
             pltpu.VMEM((slots, width, width), BF),
             pltpu.VMEM((nvec, own), BF),
             pltpu.VMEM((1, own), F32),
@@ -269,12 +279,15 @@
             pltpu.VMEM((nchip * sub * nvec, width), F32),
             pltpu.VMEM((nchip * sub * nvec, width), F32),
             pltpu.VMEM((nchip * sub * nvec, width), F32),
-            pltpu.VMEM((nchip, sub * nvec, width), F32),
+            pltpu.VMEM((nchip, sub * nvec, width), jnp.int16),
+            pltpu.VMEM((nchip, 1, width), F32),
+            pltpu.VMEM((nchip, sub * nvec, width), jnp.int16),
+            pltpu.VMEM((nchip, 1, width), F32),
             pltpu.VMEM((nrow * sub * nvec, width), F32),
             pltpu.VMEM((nrow, sub * nvec, width), F32),
-            dma((slots // GROUP,)), dma((7,)),
+            dma((slots // TURN,)), dma((7,)),
             dma((nrow,)), dma((nrow,)), dma((nchip,)), dma((nchip,)),
-            dma((1 + PIECES,)), dma((1 + PIECES,)), dma((nchip,)), dma((nchip,)), dma((nrow,)), dma((nrow,)),
+            dma((1 + PIECES,)), dma((1 + PIECES,)), dma((2, nchip)), dma((2, nchip)), dma((nrow,)), dma((nrow,)),
             pltpu.SemaphoreType.REGULAR((nchip,)),
         ],
         compiler_params=pltpu.CompilerParams(

time: 28.4 us -> 26.6 us (0.937)
  the two profiles are of different devices: /device:TPU:1 before, /device:TPU:129 now
where the time goes in v3:
time: 26.6 us; the launch traced here: 26.5 us
  Pallas kernels  25.2 us (95%)
  between operations  0.66 us (2%)
  local copies, waits for them, and re-layouts  0.6 us (2%)
    pallas_call x1, Pallas kernels, body(): pl.pallas_call(functools.partial(kernel, nrow, ncol), out_shape=pltpu.VME...  25.2 us
    unnamed x1, local copies, waits for them, and re-layouts  0.6 us

profile of v3, /device:TPU:129, one launch (start us, length us, event | category | flops | bytes accessed | tf_op | source)
XLA Modules:
  0.0 26.5 jit_solution(9013929883998900354)
XLA Ops:
  0.7 25.2 %shard_map.64 = bf16[8,512]{1,0:T(8,128)(2,1)S(1)} custom-call(bf16[8,512]{1,0:T(8,128)(2,1)} %vec.1, f32[1,512]{1,0:T(1,128)} %bitcast.1, bf16[1,1,256,128,128]{4,3,2,1,0:T(8,128)(2,1)} %tiles.1, s32[1,1,256]{2,1,0:T(1,128)} %rows.1, s32[1,1,256]{2,1,0:T(1,128)} %cols.1, s32[1,1]{1,0:T(1,128)S(6)} %copy.9.cnt), custom_call_target="tpu_custom_call" | custom-call | tf_op jit(solution)/shard_map/pallas_call | solution.py:259
  25.9 0.6 %copy.8 = bf16[8,512]{1,0:T(8,128)(2,1)} copy(bf16[8,512]{1,0:T(8,128)(2,1)S(1)} %shard_map.64) | data formatting | bytes 16384

commit v4 on v3

--- a/solution.py
+++ b/solution.py
@@ -9,10 +9,10 @@
 
 MESH = pl.DeviceIdType.MESH
 BF, F32 = jnp.bfloat16, jnp.float32
-GROUP = 128
-EARLY = 8
+GROUP = 256
+AHEAD = 8
 TURN = 32
-LIMIT = 32767.0
+LIMIT = 32766.0
 PIECES = 4
 
 
@@ -48,7 +48,7 @@
     nrow, ncol,
     vec, en, tiles, rows, cols, cnt, out,
     tv, flip, vbuf, ebuf, rows_s, rows_v, cols_s, cols_v, cnt_s,
-    seg, segf, slab, slabf, terms, mine, other, partner, fixed, scale, rsum, rscale, csum, crecv,
+    seg, segf, slab, slabf, terms, mine, other, partner, fixed, rsum, csum, cfixed, crecv,
     tile_sem, in_sem, seg_send, seg_recv, slab_send, slab_recv,
     pair_send, pair_recv, rs_send, rs_recv, cs_send, cs_recv, ready,
 ):
@@ -102,6 +102,13 @@
         index = lax.broadcasted_iota(jnp.int32, (count, slots), 0) + first
         return (index == targets).astype(BF)
 
+    def turn(g):
+        tile_copy(g).wait()
+        for u in range(TURN):
+            flip[g * TURN + u] = tv[g * TURN + u].T
+    def turn_all():
+        loop(0, nch, turn)
+    split = nchip // 2
     pl.semaphore_wait(barrier, nrow + chip)
 
     def seg_copy(d):
@@ -116,11 +123,7 @@
     loop(0, chip, lambda k: pl.semaphore_signal(
         ready.at[chip], inc=1, device_id=(r, k * 2 + core), device_id_type=MESH))
 
-    def turn(g):
-        tile_copy(g).wait()
-        for u in range(TURN):
-            flip[g * TURN + u] = tv[g * TURN + u].T
-    loop(0, nch, turn)
+    turn_all()
 
     pair_slab = remote(slab.at[core], slab.at[core], pair_send.at[0], pair_recv.at[0],
                        r, chip * 2 + 1 - core)
@@ -128,19 +131,23 @@
     size = sub * nvec
     piece = nchip // PIECES
 
+    def relay():
+        loop(0, chip, lambda k: slab_in(k).wait_recv())
+        pair_slab.start()
+
+    def to_later(k):
+        pl.semaphore_wait(ready.at[k], 1)
+        slab_out(k).start()
+
+    first = chip < max(nchip // 8, 1)
+    close = jnp.where(chip < split, jnp.where(first, split, nchip), jnp.minimum(chip // 2 * 2 + AHEAD, nchip))
+    loop(chip + 1, close, to_later)
+
     loop(1, nrow, lambda d: seg_copy(d).wait_recv())
     for k in range(nrow):
         block = seg[k].astype(F32)
         for s in range(sub):
             segf[k * sub + s] = block[s * nvec:(s + 1) * nvec]
-
-    def relay():
-        loop(0, chip, lambda k: slab_in(k).wait_recv())
-        pair_slab.start()
-
-    def to_later(k):
-        pl.semaphore_wait(ready.at[k], 1)
-        slab_out(k).start()
 
     def products(source, index, matrix):
         def step(g):
@@ -150,12 +157,6 @@
                     source[index[0, t]], source[index[0, t + 1]], matrix[t], matrix[t + 1])
         loop(0, slots // GROUP, step)
 
-    early = chip < max(nchip // EARLY, 1)
-    first = chip < max(nchip // 8, 1)
-    split = nchip // 2
-    @pl.when(jnp.logical_not(early))
-    def _():
-        loop(chip + 1, nchip, to_later)
     products(segf, cols_s, flip)
 
     half = nchip * sub
@@ -172,21 +173,30 @@
     collect(picks(place, (1 - core) * half, half), terms, slots, nvec, width, keep(other))
     loop(0, npiece, lambda q: pair_sum(q).start())
     collect(picks(place, core * half, half), terms, slots, nvec, width, keep(mine))
+    pl.when(chip < split)(relay)
+    loop(close, nchip, to_later)
 
     def rs_out(k):
-        to = (r, k * 2 + core)
-        return (remote(fixed.at[k], rsum.at[chip], rs_send.at[0, k], rs_recv.at[0, chip], *to),
-                remote(scale.at[k], rscale.at[chip], rs_send.at[1, k], rs_recv.at[1, chip], *to))
+        return remote(fixed.at[k, words], rsum.at[chip, words], rs_send.at[k], rs_recv.at[chip],
+                      r, k * 2 + core)
     def rs_in(k):
-        to = (r, k * 2 + core)
-        return (remote(rsum.at[k], rsum.at[k], rs_send.at[0, k], rs_recv.at[0, k], *to),
-                remote(rscale.at[k], rscale.at[k], rs_send.at[1, k], rs_recv.at[1, k], *to))
-    def rs_start(k):
-        for copy in rs_out(k):
-            copy.start()
-    def rs_wait(k):
-        for copy in rs_out(k):
-            copy.wait_send()
+        return remote(rsum.at[k, words], rsum.at[k, words], rs_send.at[k], rs_recv.at[k],
+                      r, k * 2 + core)
+
+    low = size // 2
+    words = pl.ds(0, low + 1)
+    def to_fixed(x):
+        most = jnp.max(jnp.abs(x), axis=0, keepdims=True)
+        power = jnp.ceil(jnp.log2(jnp.maximum(most, 2.0 ** -100)))
+        code = jnp.round(x * (jnp.exp2(-power) * LIMIT)).astype(jnp.int32)
+        word = jnp.left_shift(code[:low], 16) | (code[low:] & 0xFFFF)
+        return jnp.concatenate([word, power.astype(jnp.int32)], 0)
+    def from_fixed(ref):
+        word = ref[0:low, :]
+        code = jnp.concatenate([
+            jnp.right_shift(word, 16), jnp.right_shift(jnp.left_shift(word, 16), 16)], 0)
+        power = ref[low:low + 1, :].astype(F32)
+        return code.astype(F32) * (jnp.exp2(power) * (1.0 / LIMIT))
 
     def send_rows(q):
         pair_sum(q).wait_recv()
@@ -195,19 +205,11 @@
             part = pl.ds(pl.multiple_of(k * size, size), size)
             x = mine[part, :] + partner[part, :]
             mine[part, :] = x
-            most = jnp.max(jnp.abs(x), axis=0, keepdims=True)
-            some = most > 1e-30
-            fixed[k] = jnp.round(x * jnp.where(some, LIMIT / jnp.where(some, most, 1.0), 0.0)).astype(jnp.int32).astype(jnp.int16)
-            scale[k] = most * (1.0 / LIMIT)
-        loop(q * piece, jnp.minimum((q + 1) * piece, chip), rs_start)
+            fixed[k, 0:low + 1, :] = to_fixed(x)
+        loop(q * piece, jnp.minimum((q + 1) * piece, chip), lambda k: rs_out(k).start())
     loop(0, npiece, send_rows)
 
-    @pl.when(early)
-    def _():
-        loop(chip + 1, split, to_later)
-        pl.when(first)(relay)
-        loop(split, nchip, to_later)
-    pl.when(jnp.logical_not(first))(relay)
+    pl.when(chip >= split)(relay)
 
     pair_slab.wait_recv()
     for k in range(nchip):
@@ -220,9 +222,11 @@
     def keep_cols(v, x):
         csum[pl.ds(v, nb, stride=nvec), :] = x
     collect(picks(b, 0, nb), terms, slots, nvec, width, keep_cols)
+    for k in range(nrow):
+        cfixed[k, 0:low + 1, :] = to_fixed(csum[k * size:(k + 1) * size, :])
     def cs_copy(d):
-        there = pl.ds(pl.multiple_of(row_at(d) * size, size), size)
-        return remote(csum.at[there], crecv.at[d], cs_send.at[d], cs_recv.at[d], row_at(d), c)
+        k = row_at(d)
+        return remote(cfixed.at[k, words], crecv.at[d, words], cs_send.at[d], cs_recv.at[d], k, c)
     loop(1, nrow, lambda d: cs_copy(d).start())
 
     total = jnp.concatenate(
@@ -231,11 +235,10 @@
     total = total + csum[pl.ds(pl.multiple_of(r * size, size), size), :]
     def add_cols(d, x):
         cs_copy(d).wait_recv()
-        return x + crecv[d]
+        return x + from_fixed(crecv.at[d])
     def add_rows(k, x):
-        for copy in rs_in(k):
-            copy.wait_recv()
-        return x + rsum[k].astype(jnp.int32).astype(F32) * rscale[k]
+        rs_in(k).wait_recv()
+        return x + from_fixed(rsum.at[k])
     total = lax.fori_loop(1, nrow, add_cols, total)
     total = lax.fori_loop(chip + 1, nchip, add_rows, total)
     for s in range(sub):
@@ -245,7 +248,7 @@
     loop(chip + 1, nchip, lambda k: slab_out(k).wait_send())
     pair_slab.wait_send()
     loop(0, npiece, lambda q: pair_sum(q).wait_send())
-    loop(0, chip, rs_wait)
+    loop(0, chip, lambda k: rs_out(k).wait_send())
     loop(1, nrow, lambda d: cs_copy(d).wait_send())
 
 
@@ -279,15 +282,14 @@
             pltpu.VMEM((nchip * sub * nvec, width), F32),
             pltpu.VMEM((nchip * sub * nvec, width), F32),
             pltpu.VMEM((nchip * sub * nvec, width), F32),
-            pltpu.VMEM((nchip, sub * nvec, width), jnp.int16),
-            pltpu.VMEM((nchip, 1, width), F32),
-            pltpu.VMEM((nchip, sub * nvec, width), jnp.int16),
-            pltpu.VMEM((nchip, 1, width), F32),
+            pltpu.VMEM((nchip, sub * nvec // 2 + 8, width), jnp.int32),
+            pltpu.VMEM((nchip, sub * nvec // 2 + 8, width), jnp.int32),
             pltpu.VMEM((nrow * sub * nvec, width), F32),
-            pltpu.VMEM((nrow, sub * nvec, width), F32),
+            pltpu.VMEM((nrow, sub * nvec // 2 + 8, width), jnp.int32),
+            pltpu.VMEM((nrow, sub * nvec // 2 + 8, width), jnp.int32),
             dma((slots // TURN,)), dma((7,)),
             dma((nrow,)), dma((nrow,)), dma((nchip,)), dma((nchip,)),
-            dma((1 + PIECES,)), dma((1 + PIECES,)), dma((2, nchip)), dma((2, nchip)), dma((nrow,)), dma((nrow,)),
+            dma((1 + PIECES,)), dma((1 + PIECES,)), dma((nchip,)), dma((nchip,)), dma((nrow,)), dma((nrow,)),
             pltpu.SemaphoreType.REGULAR((nchip,)),
         ],
         compiler_params=pltpu.CompilerParams(

time: 26.6 us -> 25.4 us (0.955)
  the two profiles are of different devices: /device:TPU:129 before, /device:TPU:1 now
where the time goes in v4:
time: 25.4 us; the launch traced here: 25.3 us
  Pallas kernels  24 us (94%)
  between operations  0.66 us (3%)
  local copies, waits for them, and re-layouts  0.6 us (2%)
    pallas_call x1, Pallas kernels, body(): pl.pallas_call(functools.partial(kernel, nrow, ncol), out_shape=pltpu.VME...  24 us
    unnamed x1, local copies, waits for them, and re-layouts  0.6 us

profile of v4, /device:TPU:1, one launch (start us, length us, event | category | flops | bytes accessed | tf_op | source)
XLA Modules:
  0.0 25.3 jit_solution(11855175834297077161)
XLA Ops:
  0.7 24.0 %shard_map.64 = bf16[8,512]{1,0:T(8,128)(2,1)S(1)} custom-call(bf16[8,512]{1,0:T(8,128)(2,1)} %vec.1, f32[1,512]{1,0:T(1,128)} %bitcast.1, bf16[1,1,256,128,128]{4,3,2,1,0:T(8,128)(2,1)} %tiles.1, s32[1,1,256]{2,1,0:T(1,128)} %rows.1, s32[1,1,256]{2,1,0:T(1,128)} %cols.1, s32[1,1]{1,0:T(1,128)S(6)} %copy.9.cnt), custom_call_target="tpu_custom_call" | custom-call | tf_op jit(solution)/shard_map/pallas_call | solution.py:262
  24.7 0.6 %copy.8 = bf16[8,512]{1,0:T(8,128)(2,1)} copy(bf16[8,512]{1,0:T(8,128)(2,1)S(1)} %shard_map.64) | data formatting | bytes 16384

commit v5 on v4

--- a/solution.py
+++ b/solution.py
@@ -10,7 +10,6 @@
 MESH = pl.DeviceIdType.MESH
 BF, F32 = jnp.bfloat16, jnp.float32
 GROUP = 256
-AHEAD = 8
 TURN = 32
 LIMIT = 32766.0
 PIECES = 4
@@ -40,7 +39,7 @@
         term = terms[pl.ds(v, slots, stride=nvec), :]
         high = term.astype(BF)
         low = (term - high.astype(F32)).astype(BF)
-        out = jnp.dot(picks, jnp.concatenate([high, low], 1), preferred_element_type=F32)
+        out = jnp.dot(picks[...], jnp.concatenate([high, low], 1), preferred_element_type=F32)
         store(v, out[:, :width] + out[:, width:])
 
 
@@ -48,7 +47,7 @@
     nrow, ncol,
     vec, en, tiles, rows, cols, cnt, out,
     tv, flip, vbuf, ebuf, rows_s, rows_v, cols_s, cols_v, cnt_s,
-    seg, segf, slab, slabf, terms, mine, other, partner, fixed, rsum, csum, cfixed, crecv,
+    pick_other, pick_mine, pick_cols, seg, segf, slab, slabf, terms, mine, other, partner, fixed, rsum, csum, cfixed, crecv,
     tile_sem, in_sem, seg_send, seg_recv, slab_send, slab_recv,
     pair_send, pair_recv, rs_send, rs_recv, cs_send, cs_recv, ready,
 ):
@@ -65,8 +64,8 @@
     barrier = pltpu.get_barrier_semaphore()
     def greet(row, col):
         pl.semaphore_signal(barrier, inc=1, device_id=(row, col), device_id_type=MESH)
+    loop(1, nrow, lambda d: greet(row_at(d), c))
     greet(r, chip * 2 + 1 - core)
-    loop(1, nrow, lambda d: greet(row_at(d), c))
     loop(chip + 1, nchip, lambda k: greet(r, k * 2 + core))
 
     nch = slots // TURN
@@ -84,23 +83,12 @@
         copy.start()
     loop(0, nch, lambda g: tile_copy(g).start())
 
-    for copy in small:
-        copy.wait()
+    small[0].wait()
     own = jnp.concatenate(
         [vbuf[:, s * width:(s + 1) * width].astype(F32) for s in range(sub)], 0
     )
     seg[r] = own.astype(BF)
     slab[core, chip] = own.astype(BF)
-
-    live = lax.broadcasted_iota(jnp.int32, (1, slots), 1) < cnt_s[0, 0]
-    a, b = rows_v[...], cols_v[...]
-    place = (a // sub % 2) * (nchip * sub) + (a // (2 * sub)) * sub + a % sub
-    place = jnp.where(live, place, -1)
-    b = jnp.where(live, b, -1)
-
-    def picks(targets, first, count):
-        index = lax.broadcasted_iota(jnp.int32, (count, slots), 0) + first
-        return (index == targets).astype(BF)
 
     def turn(g):
         tile_copy(g).wait()
@@ -119,15 +107,35 @@
     def slab_in(k):
         return remote(slab.at[core, k], slab.at[core, k], slab_send.at[k], slab_recv.at[k],
                       r, k * 2 + core)
-    loop(1, nrow, lambda d: seg_copy(d).start())
+    def seg_start(k):
+        @pl.when(k != r)
+        def _():
+            seg_copy(lax.rem(k + nrow - r, nrow)).start()
+    loop(0, nrow, seg_start)
     loop(0, chip, lambda k: pl.semaphore_signal(
         ready.at[chip], inc=1, device_id=(r, k * 2 + core), device_id_type=MESH))
 
+    for copy in small[1:]:
+        copy.wait()
+    live = lax.broadcasted_iota(jnp.int32, (1, slots), 1) < cnt_s[0, 0]
+    a, b = rows_v[...], cols_v[...]
+    place = (a // sub % 2) * (nchip * sub) + (a // (2 * sub)) * sub + a % sub
+    place = jnp.where(live, place, -1)
+    b = jnp.where(live, b, -1)
+
+    def picks(targets, first, count):
+        index = lax.broadcasted_iota(jnp.int32, (count, slots), 0) + first
+        return (index == targets).astype(BF)
+    half = nchip * sub
+    nb = nrow * sub
+    pick_other[...] = picks(place, (1 - core) * half, half)
+    pick_mine[...] = picks(place, core * half, half)
+    pick_cols[...] = picks(b, 0, nb)
+
     turn_all()
 
     pair_slab = remote(slab.at[core], slab.at[core], pair_send.at[0], pair_recv.at[0],
                        r, chip * 2 + 1 - core)
-    nb = nrow * sub
     size = sub * nvec
     piece = nchip // PIECES
 
@@ -140,7 +148,7 @@
         slab_out(k).start()
 
     first = chip < max(nchip // 8, 1)
-    close = jnp.where(chip < split, jnp.where(first, split, nchip), jnp.minimum(chip // 2 * 2 + AHEAD, nchip))
+    close = jnp.where(first, split, nchip)
     loop(chip + 1, close, to_later)
 
     loop(1, nrow, lambda d: seg_copy(d).wait_recv())
@@ -159,7 +167,6 @@
 
     products(segf, cols_s, flip)
 
-    half = nchip * sub
     def keep(ref):
         def store(v, x):
             ref[pl.ds(v, half, stride=nvec), :] = x
@@ -170,9 +177,9 @@
         return remote(other.at[part], partner.at[part], pair_send.at[1 + q], pair_recv.at[1 + q],
                       r, chip * 2 + 1 - core)
     npiece = chip // piece + 1
-    collect(picks(place, (1 - core) * half, half), terms, slots, nvec, width, keep(other))
+    collect(pick_other, terms, slots, nvec, width, keep(other))
     loop(0, npiece, lambda q: pair_sum(q).start())
-    collect(picks(place, core * half, half), terms, slots, nvec, width, keep(mine))
+    collect(pick_mine, terms, slots, nvec, width, keep(mine))
     pl.when(chip < split)(relay)
     loop(close, nchip, to_later)
 
@@ -221,13 +228,24 @@
     products(slabf, rows_s, tv)
     def keep_cols(v, x):
         csum[pl.ds(v, nb, stride=nvec), :] = x
-    collect(picks(b, 0, nb), terms, slots, nvec, width, keep_cols)
+    collect(pick_cols, terms, slots, nvec, width, keep_cols)
     for k in range(nrow):
         cfixed[k, 0:low + 1, :] = to_fixed(csum[k * size:(k + 1) * size, :])
     def cs_copy(d):
         k = row_at(d)
         return remote(cfixed.at[k, words], crecv.at[d, words], cs_send.at[d], cs_recv.at[d], k, c)
-    loop(1, nrow, lambda d: cs_copy(d).start())
+    def cs_start(k):
+        @pl.when(k != r)
+        def _():
+            cs_copy(lax.rem(k + nrow - r, nrow)).start()
+    loop(0, nrow, cs_start)
+
+    loop(1, nrow, lambda d: seg_copy(d).wait_send())
+    loop(chip + 1, nchip, lambda k: slab_out(k).wait_send())
+    pair_slab.wait_send()
+    loop(0, npiece, lambda q: pair_sum(q).wait_send())
+    loop(0, chip, lambda k: rs_out(k).wait_send())
+    loop(1, nrow, lambda d: cs_copy(d).wait_send())
 
     total = jnp.concatenate(
         [own[s * nvec:(s + 1) * nvec] * ebuf[:, s * width:(s + 1) * width] for s in range(sub)], 0)
@@ -240,16 +258,11 @@
         rs_in(k).wait_recv()
         return x + from_fixed(rsum.at[k])
     total = lax.fori_loop(1, nrow, add_cols, total)
-    total = lax.fori_loop(chip + 1, nchip, add_rows, total)
+    total = lax.fori_loop(chip + 1, split, add_rows, total)
+    total = lax.fori_loop(0, jnp.minimum(split, nchip - 1 - chip),
+                          lambda i, x: add_rows(nchip - 1 - i, x), total)
     for s in range(sub):
         out[:, s * width:(s + 1) * width] = total[s * nvec:(s + 1) * nvec].astype(BF)
-
-    loop(1, nrow, lambda d: seg_copy(d).wait_send())
-    loop(chip + 1, nchip, lambda k: slab_out(k).wait_send())
-    pair_slab.wait_send()
-    loop(0, npiece, lambda q: pair_sum(q).wait_send())
-    loop(0, chip, lambda k: rs_out(k).wait_send())
-    loop(1, nrow, lambda d: cs_copy(d).wait_send())
 
 
 def body(vectors, energies, tiles, tile_rows, tile_cols, counts):
@@ -274,6 +287,9 @@
             pltpu.SMEM((1, slots), jnp.int32),
             pltpu.VMEM((1, slots), jnp.int32),
             pltpu.SMEM((1, 1), jnp.int32),
+            pltpu.VMEM((nchip * sub, slots), BF),
+            pltpu.VMEM((nchip * sub, slots), BF),
+            pltpu.VMEM((nrow * sub, slots), BF),
             pltpu.VMEM((nrow, sub * nvec, width), BF),
             pltpu.VMEM((nrow * sub, nvec, width), F32),
             pltpu.VMEM((2, nchip, sub * nvec, width), BF),

time: 25.4 us -> 25.3 us (level)
  no operation moved by 1% of the time
where the time goes in v5:
time: 25.3 us; the launch traced here: 25.1 us
  Pallas kernels  23.9 us (94%)
  between operations  0.66 us (3%)
  local copies, waits for them, and re-layouts  0.6 us (2%)
    pallas_call x1, Pallas kernels, body(): pl.pallas_call(functools.partial(kernel, nrow, ncol), out_shape=pltpu.VME...  23.9 us
    unnamed x1, local copies, waits for them, and re-layouts  0.6 us

profile of v5, /device:TPU:1, one launch (start us, length us, event | category | flops | bytes accessed | tf_op | source)
XLA Modules:
  0.0 25.1 jit_solution(8959329456284817898)
XLA Ops:
  0.7 23.9 %shard_map.64 = bf16[8,512]{1,0:T(8,128)(2,1)S(1)} custom-call(bf16[8,512]{1,0:T(8,128)(2,1)} %vec.1, f32[1,512]{1,0:T(1,128)} %bitcast.1, bf16[1,1,256,128,128]{4,3,2,1,0:T(8,128)(2,1)} %tiles.1, s32[1,1,256]{2,1,0:T(1,128)} %rows.1, s32[1,1,256]{2,1,0:T(1,128)} %cols.1, s32[1,1]{1,0:T(1,128)S(6)} %copy.9.cnt), custom_call_target="tpu_custom_call" | custom-call | tf_op jit(solution)/shard_map/pallas_call | solution.py:275
  24.5 0.6 %copy.8 = bf16[8,512]{1,0:T(8,128)(2,1)} copy(bf16[8,512]{1,0:T(8,128)(2,1)S(1)} %shard_map.64) | data formatting | bytes 16384

commit v6 on v5

--- a/solution.py
+++ b/solution.py
@@ -11,7 +11,7 @@
 BF, F32 = jnp.bfloat16, jnp.float32
 GROUP = 256
 TURN = 32
-LIMIT = 32766.0
+LIMIT = 32512.0
 PIECES = 4
 
 

time: 25.3 us -> 25.3 us (level)
  no operation moved by 1% of the time
where the time goes in v6:
time: 25.3 us; the launch traced here: 25.1 us
  Pallas kernels  23.9 us (94%)
  between operations  0.66 us (3%)
  local copies, waits for them, and re-layouts  0.6 us (2%)
    pallas_call x1, Pallas kernels, body(): pl.pallas_call(functools.partial(kernel, nrow, ncol), out_shape=pltpu.VME...  23.9 us
    unnamed x1, local copies, waits for them, and re-layouts  0.6 us

profile of v6, /device:TPU:1, one launch (start us, length us, event | category | flops | bytes accessed | tf_op | source)
XLA Modules:
  0.0 25.1 jit_solution(17685783368666974833)
XLA Ops:
  0.7 23.9 %shard_map.64 = bf16[8,512]{1,0:T(8,128)(2,1)S(1)} custom-call(bf16[8,512]{1,0:T(8,128)(2,1)} %vec.1, f32[1,512]{1,0:T(1,128)} %bitcast.1, bf16[1,1,256,128,128]{4,3,2,1,0:T(8,128)(2,1)} %tiles.1, s32[1,1,256]{2,1,0:T(1,128)} %rows.1, s32[1,1,256]{2,1,0:T(1,128)} %cols.1, s32[1,1]{1,0:T(1,128)S(6)} %copy.9.cnt), custom_call_target="tpu_custom_call" | custom-call | tf_op jit(solution)/shard_map/pallas_call | solution.py:275
  24.5 0.6 %copy.8 = bf16[8,512]{1,0:T(8,128)(2,1)} copy(bf16[8,512]{1,0:T(8,128)(2,1)S(1)} %shard_map.64) | data formatting | bytes 16384

commit v7 on v6

--- a/solution.py
+++ b/solution.py
@@ -10,6 +10,7 @@
 MESH = pl.DeviceIdType.MESH
 BF, F32 = jnp.bfloat16, jnp.float32
 GROUP = 256
+MUTUAL = 2
 TURN = 32
 LIMIT = 32512.0
 PIECES = 4
@@ -67,6 +68,9 @@
     loop(1, nrow, lambda d: greet(row_at(d), c))
     greet(r, chip * 2 + 1 - core)
     loop(chip + 1, nchip, lambda k: greet(r, k * 2 + core))
+    split = nchip // 2
+    mutual = (r < MUTUAL) & (chip >= split)
+    loop(jnp.where(mutual, split, chip), chip, lambda k: greet(r, k * 2 + core))
 
     nch = slots // TURN
     def tile_copy(g):
@@ -96,8 +100,7 @@
             flip[g * TURN + u] = tv[g * TURN + u].T
     def turn_all():
         loop(0, nch, turn)
-    split = nchip // 2
-    pl.semaphore_wait(barrier, nrow + chip)
+    pl.semaphore_wait(barrier, nrow + jnp.where(mutual, nchip - 1, chip))
 
     def seg_copy(d):
         return remote(seg.at[r], seg.at[r], seg_send.at[d], seg_recv.at[d], row_at(d), c)
@@ -112,7 +115,8 @@
         def _():
             seg_copy(lax.rem(k + nrow - r, nrow)).start()
     loop(0, nrow, seg_start)
-    loop(0, chip, lambda k: pl.semaphore_signal(
+    loop(jnp.where(mutual, chip + 1, nchip), nchip, lambda k: slab_out(k).start())
+    loop(0, jnp.where(mutual, split, chip), lambda k: pl.semaphore_signal(
         ready.at[chip], inc=1, device_id=(r, k * 2 + core), device_id_type=MESH))
 
     for copy in small[1:]:
@@ -149,13 +153,17 @@
 
     first = chip < max(nchip // 8, 1)
     close = jnp.where(first, split, nchip)
-    loop(chip + 1, close, to_later)
-
-    loop(1, nrow, lambda d: seg_copy(d).wait_recv())
-    for k in range(nrow):
+    loop(jnp.where(mutual, nchip, chip + 1), close, to_later)
+
+    def spread_seg(k):
         block = seg[k].astype(F32)
         for s in range(sub):
             segf[k * sub + s] = block[s * nvec:(s + 1) * nvec]
+    spread_seg(r)
+    def seg_arrives(d):
+        seg_copy(d).wait_recv()
+        spread_seg(lax.rem(r + nrow - d, nrow))
+    loop(1, nrow, seg_arrives)
 
     def products(source, index, matrix):
         def step(g):
@@ -218,12 +226,14 @@
 
     pl.when(chip >= split)(relay)
 
-    pair_slab.wait_recv()
-    for k in range(nchip):
-        for m in range(2):
+    def spread_slab(m):
+        for k in range(nchip):
             block = slab[m, k].astype(F32)
             for s in range(sub):
                 slabf[(k * 2 + m) * sub + s] = block[s * nvec:(s + 1) * nvec]
+    spread_slab(core)
+    pair_slab.wait_recv()
+    spread_slab(1 - core)
 
     products(slabf, rows_s, tv)
     def keep_cols(v, x):

time: 25.3 us -> 25.3 us (level)
  no operation moved by 1% of the time
where the time goes in v7:
time: 25.3 us; the launch traced here: 25.1 us
  Pallas kernels  23.9 us (94%)
  between operations  0.66 us (3%)
  local copies, waits for them, and re-layouts  0.6 us (2%)
    pallas_call x1, Pallas kernels, body(): pl.pallas_call(functools.partial(kernel, nrow, ncol), out_shape=pltpu.VME...  23.9 us
    unnamed x1, local copies, waits for them, and re-layouts  0.6 us

profile of v7, /device:TPU:1, one launch (start us, length us, event | category | flops | bytes accessed | tf_op | source)
XLA Modules:
  0.0 25.1 jit_solution(8284178320314095230)
XLA Ops:
  0.7 23.9 %shard_map.64 = bf16[8,512]{1,0:T(8,128)(2,1)S(1)} custom-call(bf16[8,512]{1,0:T(8,128)(2,1)} %vec.1, f32[1,512]{1,0:T(1,128)} %bitcast.1, bf16[1,1,256,128,128]{4,3,2,1,0:T(8,128)(2,1)} %tiles.1, s32[1,1,256]{2,1,0:T(1,128)} %rows.1, s32[1,1,256]{2,1,0:T(1,128)} %cols.1, s32[1,1]{1,0:T(1,128)S(6)} %copy.9.cnt), custom_call_target="tpu_custom_call" | custom-call | tf_op jit(solution)/shard_map/pallas_call | solution.py:285
  24.5 0.6 %copy.8 = bf16[8,512]{1,0:T(8,128)(2,1)} copy(bf16[8,512]{1,0:T(8,128)(2,1)S(1)} %shard_map.64) | data formatting | bytes 16384
